TPU v7x, 128 devices: a whole 4x4x4 slice. The times are simulated.
128 devices in a mesh: ctx: 32 (over y_hi, x, z), head: 4 (over y_lo, core).
Axes of the slice: x: 4, y: 4 (y_hi: 2, y_lo: 2; y = y_hi * 2 + y_lo), z: 4, core: 2. Of those that a mesh axis runs over, the one named last changes fastest.
Arguments:
- query: bfloat16 [8192, 3072], P(('ctx', 'head')), may hold values from -8 to 8
- key: bfloat16 [8192, 512], P(('ctx', 'head')), may hold values from -8 to 8
- value: bfloat16 [8192, 512], P(('ctx', 'head')), may hold values from -24 to 24
- residual: bfloat16 [8192, 6144], P(('ctx', 'head')), may hold values from -4 to 4
- out_weight: bfloat16 [3072, 6144], P('head'), may hold values from -0.109375 to 0.109375
- gate_table: float32 [4, 6144], replicated, may hold values from 0.5 to 2
- span_of_shard: int32 [32], replicated, may hold values from 0 to 3, as said below
- noise_level: int32 [4], replicated, may hold values from 0 to 3
- visible: int32 [4, 4], replicated, may hold values from 0 to 1, as said below
Outputs:
- mixed: bfloat16 [8192, 6144], P(('ctx', 'head'))
Inputs may be any that keep to these rules, and one draw needn't show every extreme that they name: `span_of_shard`: Non-decreasing along the shards, starts at 0, ends at 3, and every span holds at least one shard. `visible`: the diagonal is 1 and every entry above it is 0.
All inputs are finite; a program needn't handle non-finite values.
Results may differ from a plain program's by a relative error of at most 0.015.
Values may be sent and summed in bfloat16 or wider, within the bound.
A program may use at most 64 MiB of HBM per device.

v0:
```python
import math

import jax
import jax.numpy as jnp
from jax import lax
from jax.sharding import PartitionSpec as P

HEADS = 24
KV_HEADS = 4
HD = 128


NEG = -1e30


def block_update(carry, keys, values, key_span, queries, query_vis, scale):
    m_old, l_old, acc = carry
    scores = jnp.einsum("qagd,kad->agqk", queries, keys, preferred_element_type=jnp.float32) * scale
    onehot = (key_span[:, None] == jnp.arange(query_vis.shape[1], dtype=jnp.int32)[None, :]).astype(
        jnp.float32
    )
    allowed = (jnp.dot(query_vis, onehot.T) > 0.5)[None, None]
    masked = jnp.where(allowed, scores, NEG)
    m_new = jnp.maximum(m_old, jnp.max(masked, axis=3))
    weights = jnp.where(allowed, jnp.exp(masked - m_new[..., None]), 0.0)
    factor = jnp.exp(m_old - m_new)
    l_new = l_old * factor + jnp.sum(weights, axis=3)
    acc = acc * factor[..., None] + jnp.einsum(
        "agqk,kad->agqd", weights.astype(jnp.bfloat16), values, preferred_element_type=jnp.float32
    )
    return (m_new, l_new, acc)


def fold_keys(carry, piece, queries, query_vis, span_map, tok_ctx, scale):
    keys, values = piece
    rows = keys.shape[0]
    kv_here = queries.shape[1]
    width = queries.shape[3]
    size = math.gcd(rows, 1024)
    count = rows // size
    key_shard = jnp.arange(rows, dtype=jnp.int32) // tok_ctx
    shard_ids = jnp.arange(span_map.shape[0], dtype=jnp.int32)
    key_span = jnp.sum(
        jnp.where(key_shard[:, None] == shard_ids[None, :], span_map[None, :], 0), axis=1
    )
    keys = keys.reshape(count, size, kv_here, width)
    values = values.reshape(count, size, kv_here, width)
    key_span = key_span.reshape(count, size)

    def update(state, block):
        return block_update(state, block[0], block[1], block[2], queries, query_vis, scale)

    def step(state, block):
        state = update(state, block)
        return (state, None)

    carry, _ = lax.scan(step, carry, (keys, values, key_span))
    return carry


def on_device(
    query, key, value, residual, out_weight, gate_table, span_of_shard, noise_level, visible
):
    ctx_size = lax.axis_size("ctx")
    ctx_index = lax.axis_index("ctx")
    shard_ids = jnp.arange(ctx_size, dtype=jnp.int32)
    span_here = jnp.sum(jnp.where(shard_ids == ctx_index, span_of_shard, 0))
    local_q, local_k, local_v = (
        lax.all_to_all(query, "head", split_axis=1, concat_axis=0, tiled=True),
        lax.all_to_all(key, "head", split_axis=1, concat_axis=0, tiled=True),
        lax.all_to_all(value, "head", split_axis=1, concat_axis=0, tiled=True),
    )
    tok_ctx = local_q.shape[0]
    share = HEADS // KV_HEADS
    heads_here = local_q.shape[1] // HD
    kv_here = heads_here // share
    row_span = jnp.full((tok_ctx,), span_here, jnp.int32)
    span_ids = jnp.arange(visible.shape[0], dtype=jnp.int32)
    row_onehot = (row_span[:, None] == span_ids[None, :]).astype(jnp.float32)
    query_vis = jnp.dot(row_onehot, visible.astype(jnp.float32))
    queries = local_q.reshape(tok_ctx, kv_here, share, HD)
    scale = 1.0 / math.sqrt(HD)
    initial = (
        jnp.full((kv_here, share, tok_ctx), NEG, jnp.float32),
        jnp.zeros((kv_here, share, tok_ctx), jnp.float32),
        jnp.zeros((kv_here, share, tok_ctx, HD), jnp.float32),
    )
    final = fold_keys(
        initial,
        (
            lax.all_gather(local_k, "ctx", axis=0, tiled=True),
            lax.all_gather(local_v, "ctx", axis=0, tiled=True),
        ),
        queries,
        query_vis,
        span_of_shard,
        tok_ctx,
        scale,
    )
    attended = final[2] / final[1][..., None]
    attended = (
        jnp.transpose(attended, (2, 0, 1, 3)).reshape(tok_ctx, heads_here * HD).astype(jnp.bfloat16)
    )
    projected = lax.psum_scatter(
        jnp.dot(attended, out_weight, preferred_element_type=jnp.float32).astype(jnp.bfloat16),
        "head",
        scatter_dimension=0,
        tiled=True,
    ).astype(jnp.float32)
    level_here = jnp.sum(jnp.where(span_ids == span_here, noise_level, 0))
    level_ids = jnp.arange(gate_table.shape[0], dtype=jnp.int32)
    gate = jnp.sum(jnp.where(level_ids[:, None] == level_here, gate_table, 0.0), axis=0)
    return (residual.astype(jnp.float32) + gate[None, :] * projected).astype(jnp.bfloat16)


def solution(mesh):
    placed = (
        P(("ctx", "head"), None),
        P(("ctx", "head"), None),
        P(("ctx", "head"), None),
        P(("ctx", "head"), None),
        P("head", None),
        P(),
        P(),
        P(),
        P(),
    )
    return jax.shard_map(
        on_device, mesh=mesh, in_specs=placed, out_specs=P(("ctx", "head"), None), check_vma=False
    )
```

profile of v0, /device:TPU:1, one launch (start us, length us, event | category | flops | bytes accessed | tf_op | source)
XLA Modules:
  0.0 301.9 jit_solution(12391232383839767111)
XLA Ops:
  6.5 0.8 copy-done
  7.4 7.7 %all_to_all.54 = bf16[64,4,128]{2,0,1:T(8,128)(2,1)} all-to-all(bf16[64,4,128]{2,0,1:T(8,128)(2,1)S(1)} %copy_bitcast_fusion.2), channel_id=1, replica_groups=mesh['ctx'=32,'head'=4] {'head'}, dimensions={1} | all-to-all | bytes 131072 | tf_op jit(solution)/shard_map/all_to_all | solution.py:70
  15.2 0.9 copy_bitcast_fusion.1
  16.0 7.2 %all_to_all.55 = bf16[64,4,128]{2,0,1:T(8,128)(2,1)} all-to-all(bf16[64,4,128]{2,0,1:T(8,128)(2,1)S(1)} %copy_bitcast_fusion.1), channel_id=1, replica_groups=mesh['ctx'=32,'head'=4] {'head'}, dimensions={1} | all-to-all | bytes 131072 | tf_op jit(solution)/shard_map/all_to_all | solution.py:71
  23.2 1.8 copy.42
  25.0 4.3 %all-to-all-start.1 = ((bf16[64,4,768]{2,0,1:T(8,128)(2,1)}), bf16[64,4,768]{2,0,1:T(8,128)(2,1)S(1)}, u32[]{:S(2)}, u32[]{:S(2)}) async-start(bf16[64,4,768]{2,0,1:T(8,128)(2,1)} %bitcast.87), calls=%async_computation.1 | async-start | bytes 786432 | tf_op jit(solution)/shard_map/all_to_all | solution.py:69
  29.3 0.9 select_reduce_fusion
  30.2 1.4 fusion.33
  31.6 0.7 iota_compare_fusion.3
  32.3 0.8 fusion.27
  33.1 2.9 all-to-all-done.1
  36.0 0.5 reshape.80
  36.4 0.1 copy.33
  36.5 51.0 %all-gather.3.cloned.1.call-done = bf16[8192,128]{1,0:T(8,128)(2,1)} async-done(((bf16[256,128]{1,0:T(8,128)(2,1)}), bf16[8192,128]{1,0:T(8,128)(2,1)}) %all-gather.3.cloned.1.call-update) | async-done | bytes 2097168 | tf_op jit(solution)/shard_map/all_gather | solution.py:91
  87.5 70.9 %all-gather.5.cloned.1.call-done = bf16[8192,128]{1,0:T(8,128)(2,1)} async-done(((bf16[256,128]{1,0:T(8,128)(2,1)}), bf16[8192,128]{1,0:T(8,128)(2,1)}) %all-gather.5.cloned.1.call-update) | async-done | bytes 2097168 | tf_op jit(solution)/shard_map/all_gather | solution.py:92
  158.3 91.1 %while.15 = (s32[]{:T(128)}, f32[1,6,256]{2,1,0:T(8,128)S(1)}, f32[1,6,256]{2,1,0:T(8,128)S(1)}, f32[1,6,256,128]{3,2,1,0:T(8,128)S(1)}, s32[8,1024]{1,0:T(8,128...) while((s32[]{:T(128)}, f32[1,6,256]{2,1,0:T(8,128)S(1)}, ...), condition=%wide.region_7.8_spmd.clone, body=%wide.region_4.7_spmd.clone.sunk | while | flops 828716032 | bytes 47692952 | solution.py:57
  158.3 0.4 fusion.51
  158.7 4.7 %fusion.52 = (f32[6,256]{1,0:T(8,128)S(1)}, f32[1024,256,6]{1,0,2:T(8,128)}) fusion(pred[256,1024]{0,1:T(8,128)(4,1)S(1)} %fusion.51, bf16[256,1,6,128]{3,0,2,1:T(8,128)(2,1)S(1)} %get-tuple-element.235, bf16[8,1024,1,128]{3,1,2,0:T(8,128)(2,1)} %get-tuple-element.234, s32[]{:T(128)} %get-tuple-element.217), kind=kOutput, calls=%fused_computation.2.clone.1 | convolution fusion | flops 407370240 | bytes 7215616 | tf_op jit(solution)/shard_map/while/body/eval_jaxpr/qagd,kad->agqk/dot_general | solution.py:18
  163.5 4.1 %fusion.55 = f32[1,6,256,128]{3,2,1,0:T(8,128)S(1)} fusion(f32[1024,256,6]{1,0,2:T(8,128)} %get-tuple-element.204, f32[6,256]{1,0:T(8,128)S(1)} %bitcast.116, pred[256,1024]{0,1:T(8,128)(4,1)S(1)} %fusion.51, f32[1,6,256,128]{3,2,1,0:T(8,128)S(1)} %get-tuple-element.220, f32[6,256]{1,0:T(8,128)S(1)} %get-tuple-element.205, pred[]{:T(512)S(6)} %compare.7, ...), kind=kOutput, calls=%fused_computation.9.clone.1 | convolution fusion | flops 411107328 | bytes 8401409 | tf_op jit(solution)/shard_map/while/body/eval_jaxpr/agqk,kad->agqd/dot_general | solution.py:28
  167.6 0.6 copy-done.1
  168.2 1.5 fusion.54
  169.7 0.4 fusion.51
  170.1 4.7 %fusion.52 = (f32[6,256]{1,0:T(8,128)S(1)}, f32[1024,256,6]{1,0,2:T(8,128)}) fusion(pred[256,1024]{0,1:T(8,128)(4,1)S(1)} %fusion.51, bf16[256,1,6,128]{3,0,2,1:T(8,128)(2,1)S(1)} %get-tuple-element.235, bf16[8,1024,1,128]{3,1,2,0:T(8,128)(2,1)} %get-tuple-element.234, s32[]{:T(128)} %get-tuple-element.217), kind=kOutput, calls=%fused_computation.2.clone.1 | convolution fusion | flops 407370240 | bytes 7215616 | tf_op jit(solution)/shard_map/while/body/eval_jaxpr/qagd,kad->agqk/dot_general | solution.py:18
  174.8 4.1 %fusion.55 = f32[1,6,256,128]{3,2,1,0:T(8,128)S(1)} fusion(f32[1024,256,6]{1,0,2:T(8,128)} %get-tuple-element.204, f32[6,256]{1,0:T(8,128)S(1)} %bitcast.116, pred[256,1024]{0,1:T(8,128)(4,1)S(1)} %fusion.51, f32[1,6,256,128]{3,2,1,0:T(8,128)S(1)} %get-tuple-element.220, f32[6,256]{1,0:T(8,128)S(1)} %get-tuple-element.205, pred[]{:T(512)S(6)} %compare.7, ...), kind=kOutput, calls=%fused_computation.9.clone.1 | convolution fusion | flops 411107328 | bytes 8401409 | tf_op jit(solution)/shard_map/while/body/eval_jaxpr/agqk,kad->agqd/dot_general | solution.py:28
  179.0 0.6 copy-done.1
  179.6 1.5 fusion.54
  181.1 0.4 fusion.51
  181.5 4.7 %fusion.52 = (f32[6,256]{1,0:T(8,128)S(1)}, f32[1024,256,6]{1,0,2:T(8,128)}) fusion(pred[256,1024]{0,1:T(8,128)(4,1)S(1)} %fusion.51, bf16[256,1,6,128]{3,0,2,1:T(8,128)(2,1)S(1)} %get-tuple-element.235, bf16[8,1024,1,128]{3,1,2,0:T(8,128)(2,1)} %get-tuple-element.234, s32[]{:T(128)} %get-tuple-element.217), kind=kOutput, calls=%fused_computation.2.clone.1 | convolution fusion | flops 407370240 | bytes 7215616 | tf_op jit(solution)/shard_map/while/body/eval_jaxpr/qagd,kad->agqk/dot_general | solution.py:18
  186.2 4.1 %fusion.55 = f32[1,6,256,128]{3,2,1,0:T(8,128)S(1)} fusion(f32[1024,256,6]{1,0,2:T(8,128)} %get-tuple-element.204, f32[6,256]{1,0:T(8,128)S(1)} %bitcast.116, pred[256,1024]{0,1:T(8,128)(4,1)S(1)} %fusion.51, f32[1,6,256,128]{3,2,1,0:T(8,128)S(1)} %get-tuple-element.220, f32[6,256]{1,0:T(8,128)S(1)} %get-tuple-element.205, pred[]{:T(512)S(6)} %compare.7, ...), kind=kOutput, calls=%fused_computation.9.clone.1 | convolution fusion | flops 411107328 | bytes 8401409 | tf_op jit(solution)/shard_map/while/body/eval_jaxpr/agqk,kad->agqd/dot_general | solution.py:28
  190.4 0.6 copy-done.1
  191.0 1.5 fusion.54
  192.5 0.4 fusion.51
  192.9 4.7 %fusion.52 = (f32[6,256]{1,0:T(8,128)S(1)}, f32[1024,256,6]{1,0,2:T(8,128)}) fusion(pred[256,1024]{0,1:T(8,128)(4,1)S(1)} %fusion.51, bf16[256,1,6,128]{3,0,2,1:T(8,128)(2,1)S(1)} %get-tuple-element.235, bf16[8,1024,1,128]{3,1,2,0:T(8,128)(2,1)} %get-tuple-element.234, s32[]{:T(128)} %get-tuple-element.217), kind=kOutput, calls=%fused_computation.2.clone.1 | convolution fusion | flops 407370240 | bytes 7215616 | tf_op jit(solution)/shard_map/while/body/eval_jaxpr/qagd,kad->agqk/dot_general | solution.py:18
  197.6 4.1 %fusion.55 = f32[1,6,256,128]{3,2,1,0:T(8,128)S(1)} fusion(f32[1024,256,6]{1,0,2:T(8,128)} %get-tuple-element.204, f32[6,256]{1,0:T(8,128)S(1)} %bitcast.116, pred[256,1024]{0,1:T(8,128)(4,1)S(1)} %fusion.51, f32[1,6,256,128]{3,2,1,0:T(8,128)S(1)} %get-tuple-element.220, f32[6,256]{1,0:T(8,128)S(1)} %get-tuple-element.205, pred[]{:T(512)S(6)} %compare.7, ...), kind=kOutput, calls=%fused_computation.9.clone.1 | convolution fusion | flops 411107328 | bytes 8401409 | tf_op jit(solution)/shard_map/while/body/eval_jaxpr/agqk,kad->agqd/dot_general | solution.py:28
  201.8 0.6 copy-done.1
  202.3 1.5 fusion.54
  203.9 0.4 fusion.51
  204.3 4.7 %fusion.52 = (f32[6,256]{1,0:T(8,128)S(1)}, f32[1024,256,6]{1,0,2:T(8,128)}) fusion(pred[256,1024]{0,1:T(8,128)(4,1)S(1)} %fusion.51, bf16[256,1,6,128]{3,0,2,1:T(8,128)(2,1)S(1)} %get-tuple-element.235, bf16[8,1024,1,128]{3,1,2,0:T(8,128)(2,1)} %get-tuple-element.234, s32[]{:T(128)} %get-tuple-element.217), kind=kOutput, calls=%fused_computation.2.clone.1 | convolution fusion | flops 407370240 | bytes 7215616 | tf_op jit(solution)/shard_map/while/body/eval_jaxpr/qagd,kad->agqk/dot_general | solution.py:18
  209.0 4.1 %fusion.55 = f32[1,6,256,128]{3,2,1,0:T(8,128)S(1)} fusion(f32[1024,256,6]{1,0,2:T(8,128)} %get-tuple-element.204, f32[6,256]{1,0:T(8,128)S(1)} %bitcast.116, pred[256,1024]{0,1:T(8,128)(4,1)S(1)} %fusion.51, f32[1,6,256,128]{3,2,1,0:T(8,128)S(1)} %get-tuple-element.220, f32[6,256]{1,0:T(8,128)S(1)} %get-tuple-element.205, pred[]{:T(512)S(6)} %compare.7, ...), kind=kOutput, calls=%fused_computation.9.clone.1 | convolution fusion | flops 411107328 | bytes 8401409 | tf_op jit(solution)/shard_map/while/body/eval_jaxpr/agqk,kad->agqd/dot_general | solution.py:28
  213.2 0.6 copy-done.1
  213.7 1.5 fusion.54
  215.3 0.4 fusion.51
  215.7 4.7 %fusion.52 = (f32[6,256]{1,0:T(8,128)S(1)}, f32[1024,256,6]{1,0,2:T(8,128)}) fusion(pred[256,1024]{0,1:T(8,128)(4,1)S(1)} %fusion.51, bf16[256,1,6,128]{3,0,2,1:T(8,128)(2,1)S(1)} %get-tuple-element.235, bf16[8,1024,1,128]{3,1,2,0:T(8,128)(2,1)} %get-tuple-element.234, s32[]{:T(128)} %get-tuple-element.217), kind=kOutput, calls=%fused_computation.2.clone.1 | convolution fusion | flops 407370240 | bytes 7215616 | tf_op jit(solution)/shard_map/while/body/eval_jaxpr/qagd,kad->agqk/dot_general | solution.py:18
  220.4 4.1 %fusion.55 = f32[1,6,256,128]{3,2,1,0:T(8,128)S(1)} fusion(f32[1024,256,6]{1,0,2:T(8,128)} %get-tuple-element.204, f32[6,256]{1,0:T(8,128)S(1)} %bitcast.116, pred[256,1024]{0,1:T(8,128)(4,1)S(1)} %fusion.51, f32[1,6,256,128]{3,2,1,0:T(8,128)S(1)} %get-tuple-element.220, f32[6,256]{1,0:T(8,128)S(1)} %get-tuple-element.205, pred[]{:T(512)S(6)} %compare.7, ...), kind=kOutput, calls=%fused_computation.9.clone.1 | convolution fusion | flops 411107328 | bytes 8401409 | tf_op jit(solution)/shard_map/while/body/eval_jaxpr/agqk,kad->agqd/dot_general | solution.py:28
  224.6 0.6 copy-done.1
  225.1 1.5 fusion.54
  226.7 0.4 fusion.51
  227.1 4.7 %fusion.52 = (f32[6,256]{1,0:T(8,128)S(1)}, f32[1024,256,6]{1,0,2:T(8,128)}) fusion(pred[256,1024]{0,1:T(8,128)(4,1)S(1)} %fusion.51, bf16[256,1,6,128]{3,0,2,1:T(8,128)(2,1)S(1)} %get-tuple-element.235, bf16[8,1024,1,128]{3,1,2,0:T(8,128)(2,1)} %get-tuple-element.234, s32[]{:T(128)} %get-tuple-element.217), kind=kOutput, calls=%fused_computation.2.clone.1 | convolution fusion | flops 407370240 | bytes 7215616 | tf_op jit(solution)/shard_map/while/body/eval_jaxpr/qagd,kad->agqk/dot_general | solution.py:18
  231.8 4.1 %fusion.55 = f32[1,6,256,128]{3,2,1,0:T(8,128)S(1)} fusion(f32[1024,256,6]{1,0,2:T(8,128)} %get-tuple-element.204, f32[6,256]{1,0:T(8,128)S(1)} %bitcast.116, pred[256,1024]{0,1:T(8,128)(4,1)S(1)} %fusion.51, f32[1,6,256,128]{3,2,1,0:T(8,128)S(1)} %get-tuple-element.220, f32[6,256]{1,0:T(8,128)S(1)} %get-tuple-element.205, pred[]{:T(512)S(6)} %compare.7, ...), kind=kOutput, calls=%fused_computation.9.clone.1 | convolution fusion | flops 411107328 | bytes 8401409 | tf_op jit(solution)/shard_map/while/body/eval_jaxpr/agqk,kad->agqd/dot_general | solution.py:28
  236.0 0.6 copy-done.1
  236.5 1.5 fusion.54
  238.1 0.4 fusion.51
  238.5 4.7 %fusion.52 = (f32[6,256]{1,0:T(8,128)S(1)}, f32[1024,256,6]{1,0,2:T(8,128)}) fusion(pred[256,1024]{0,1:T(8,128)(4,1)S(1)} %fusion.51, bf16[256,1,6,128]{3,0,2,1:T(8,128)(2,1)S(1)} %get-tuple-element.235, bf16[8,1024,1,128]{3,1,2,0:T(8,128)(2,1)} %get-tuple-element.234, s32[]{:T(128)} %get-tuple-element.217), kind=kOutput, calls=%fused_computation.2.clone.1 | convolution fusion | flops 407370240 | bytes 7215616 | tf_op jit(solution)/shard_map/while/body/eval_jaxpr/qagd,kad->agqk/dot_general | solution.py:18
  243.2 4.1 %fusion.55 = f32[1,6,256,128]{3,2,1,0:T(8,128)S(1)} fusion(f32[1024,256,6]{1,0,2:T(8,128)} %get-tuple-element.204, f32[6,256]{1,0:T(8,128)S(1)} %bitcast.116, pred[256,1024]{0,1:T(8,128)(4,1)S(1)} %fusion.51, f32[1,6,256,128]{3,2,1,0:T(8,128)S(1)} %get-tuple-element.220, f32[6,256]{1,0:T(8,128)S(1)} %get-tuple-element.205, pred[]{:T(512)S(6)} %compare.7, ...), kind=kOutput, calls=%fused_computation.9.clone.1 | convolution fusion | flops 411107328 | bytes 8401409 | tf_op jit(solution)/shard_map/while/body/eval_jaxpr/agqk,kad->agqd/dot_general | solution.py:28
  247.4 0.6 copy-done.1
  247.9 1.5 fusion.54
  249.5 0.3 copy.34
  249.7 0.1 divide_convert_fusion
  249.9 7.8 %convolution_convert_fusion = bf16[256,6144]{1,0:T(8,128)(2,1)} fusion(bf16[256,768]{0,1:T(8,128)(2,1)S(1)} %bitcast.118, bf16[768,6144]{1,0:T(8,128)(2,1)} %param.15), kind=kOutput, calls=%fused_computation.32 | convolution fusion | flops 2417491968 | bytes 12976128 | tf_op jit(solution)/shard_map/dot_general | solution.py:105
  257.7 1.3 fusion.34
  259.0 0.6 iota_compare_fusion.4
  259.7 0.1 select_reduce_fusion.1
  259.8 33.3 %reduce-scatter.2.cloned.1.call-done = bf16[64,6144]{1,0:T(8,128)(2,1)} async-done(((bf16[256,6144]{1,0:T(8,128)(2,1)}), bf16[64,6144]{1,0:T(8,128)(2,1)}) %reduce-scatter.2.cloned.1.call-update) | async-done | bytes 786448 | tf_op jit(solution)/shard_map/reduce_scatter | solution.py:104
  293.1 2.2 add_convert_fusion
  (59 shorter events, 0.4 us)
Async XLA Ops:
  6.5 0.8 copy-start
  6.5 80.9 %all-gather.3.cloned.1.call-start = ((), (), s32[]{:S(2)}) async-start(), calls=%async_computation.4 | async-start | bytes 2162688 | tf_op jit(solution)/shard_map/all_gather | solution.py:91
  15.1 143.2 %all-gather.5.cloned.1.call-start = ((), (), s32[]{:S(2)}) async-start(), calls=%async_computation.5 | async-start | bytes 2162688 | tf_op jit(solution)/shard_map/all_gather | solution.py:92
  25.0 11.0 %all-to-all-start.1 = ((bf16[64,4,768]{2,0,1:T(8,128)(2,1)}), bf16[64,4,768]{2,0,1:T(8,128)(2,1)S(1)}, u32[]{:S(2)}, u32[]{:S(2)}) async-start(bf16[64,4,768]{2,0,1:T(8,128)(2,1)} %bitcast.87), calls=%async_computation.1 | async-start | bytes 786432 | tf_op jit(solution)/shard_map/all_to_all | solution.py:69
  29.3 263.8 %reduce-scatter.2.cloned.1.call-start = ((), (), s32[]{:S(2)}) async-start(), calls=%async_computation.6 | async-start | bytes 3932160 | tf_op jit(solution)/shard_map/reduce_scatter | solution.py:104
  163.5 4.7 %copy-start.1 = (f32[1024,256,6]{1,0,2:T(8,128)S(1)}, f32[1024,256,6]{1,0,2:T(8,128)}, u32[]{:S(2)}) copy-start(f32[1024,256,6]{1,0,2:T(8,128)} %get-tuple-element.204) | copy-start | bytes 18874372 | tf_op jit(solution)/shard_map/while
  174.8 4.7 %copy-start.1 = (f32[1024,256,6]{1,0,2:T(8,128)S(1)}, f32[1024,256,6]{1,0,2:T(8,128)}, u32[]{:S(2)}) copy-start(f32[1024,256,6]{1,0,2:T(8,128)} %get-tuple-element.204) | copy-start | bytes 18874372 | tf_op jit(solution)/shard_map/while
  186.2 4.7 %copy-start.1 = (f32[1024,256,6]{1,0,2:T(8,128)S(1)}, f32[1024,256,6]{1,0,2:T(8,128)}, u32[]{:S(2)}) copy-start(f32[1024,256,6]{1,0,2:T(8,128)} %get-tuple-element.204) | copy-start | bytes 18874372 | tf_op jit(solution)/shard_map/while
  197.6 4.7 %copy-start.1 = (f32[1024,256,6]{1,0,2:T(8,128)S(1)}, f32[1024,256,6]{1,0,2:T(8,128)}, u32[]{:S(2)}) copy-start(f32[1024,256,6]{1,0,2:T(8,128)} %get-tuple-element.204) | copy-start | bytes 18874372 | tf_op jit(solution)/shard_map/while
  209.0 4.7 %copy-start.1 = (f32[1024,256,6]{1,0,2:T(8,128)S(1)}, f32[1024,256,6]{1,0,2:T(8,128)}, u32[]{:S(2)}) copy-start(f32[1024,256,6]{1,0,2:T(8,128)} %get-tuple-element.204) | copy-start | bytes 18874372 | tf_op jit(solution)/shard_map/while
  220.4 4.7 %copy-start.1 = (f32[1024,256,6]{1,0,2:T(8,128)S(1)}, f32[1024,256,6]{1,0,2:T(8,128)}, u32[]{:S(2)}) copy-start(f32[1024,256,6]{1,0,2:T(8,128)} %get-tuple-element.204) | copy-start | bytes 18874372 | tf_op jit(solution)/shard_map/while
  231.8 4.7 %copy-start.1 = (f32[1024,256,6]{1,0,2:T(8,128)S(1)}, f32[1024,256,6]{1,0,2:T(8,128)}, u32[]{:S(2)}) copy-start(f32[1024,256,6]{1,0,2:T(8,128)} %get-tuple-element.204) | copy-start | bytes 18874372 | tf_op jit(solution)/shard_map/while
  243.2 4.7 %copy-start.1 = (f32[1024,256,6]{1,0,2:T(8,128)S(1)}, f32[1024,256,6]{1,0,2:T(8,128)}, u32[]{:S(2)}) copy-start(f32[1024,256,6]{1,0,2:T(8,128)} %get-tuple-element.204) | copy-start | bytes 18874372 | tf_op jit(solution)/shard_map/while
  249.8 7.9 %copy-start.4 = (s32[4]{0:T(128)S(1)}, s32[4]{0:T(128)}, u32[]{:S(2)}) copy-start(s32[4]{0:T(128)} %param.18) | copy-start | bytes 52
  249.8 9.9 %copy-start.3 = (f32[4,6144]{1,0:T(4,128)S(1)}, f32[4,6144]{1,0:T(4,128)}, u32[]{:S(2)}) copy-start(f32[4,6144]{1,0:T(4,128)} %param.16) | copy-start | bytes 294916
  249.8 43.3 %copy-start.2 = (bf16[64,6144]{1,0:T(8,128)(2,1)S(1)}, bf16[64,6144]{1,0:T(8,128)(2,1)}, u32[]{:S(2)}) copy-start(bf16[64,6144]{1,0:T(8,128)(2,1)} %param.14) | copy-start | bytes 2359300
Sparse Core Ops, SparseCore 0:
  15.2 72.1 all-gather.2
  90.6 67.7 all-gather.4
  257.8 35.2 reduce-scatter.1
where the time goes:
time: 303 us; the launch traced here: 302 us
  waiting for transfers between devices  158 us (52%)
  matrix products  82.5 us (27%)
  other arithmetic  19.6 us (6%)
  blocking collectives  14.9 us (5%)
  between operations  13.2 us (4%)
  local copies, waits for them, and re-layouts  8.87 us (3%)
  starting transfers between devices  4.34 us (1%)
    all_gather x1, waiting for transfers between devices, on_device(): lax.all_gather(local_v, 'ctx', axis=0, tiled=True)  70.9 us
    all_gather x1, waiting for transfers between devices, on_device(): lax.all_gather(local_k, 'ctx', axis=0, tiled=True)  51 us
    dot_general x8, matrix products, block_update(): jnp.einsum('qagd,kad->agqk', queries, keys, preferred_element_type=jnp.fl...  37.8 us
    reduce_scatter x1, waiting for transfers between devices, on_device(): lax.psum_scatter(jnp.dot(attended, out_weight, preferred_element_type=jnp...  33.3 us
    dot_general x8, matrix products, block_update(): jnp.einsum('agqk,kad->agqd', weights.astype(jnp.bfloat16), values, prefer...  33.1 us
    reduce_sum x8, other arithmetic, block_update(): l_new = l_old * factor + jnp.sum(weights, axis=3)  12.1 us
    dot_general x1, matrix products, on_device(): jnp.dot(attended, out_weight, preferred_element_type=jnp.float32)  7.84 us
    all_to_all x1, blocking collectives, on_device(): lax.all_to_all(key, 'head', split_axis=1, concat_axis=0, tiled=True)  7.71 us
  transfers between devices with their start and end apart: 4, of which 4 were waited for; matrix products, arithmetic and copies ran while one was open for 3% of the time, Pallas kernels for 0%

commit v1 on v0

v1 whole, which is shorter than its diff:
```python
import math

import jax
import jax.numpy as jnp
from jax import lax
from jax.experimental import pallas as pl
from jax.experimental.pallas import tpu as pltpu
from jax.sharding import PartitionSpec as P

HD = 128
KV_HEADS = 4
SHARE = 6
WIDTH = SHARE * HD
BLOCK = 64
ROWS = SHARE * BLOCK
D = 6144
CHUNKS = 6
CHUNK = D // CHUNKS
RING = 4
NEG = -1e30
BIG = 1e30
MESH = pl.DeviceIdType.MESH

PLACE = {
    (0, 0): 0,
    (1, 0): 1,
    (0, 1): 2,
    (3, 0): 3,
    (0, 3): 4,
    (1, 1): 5,
    (3, 3): 6,
    (3, 1): 7,
    (1, 3): 8,
    (2, 0): 9,
    (0, 2): 10,
    (2, 1): 11,
    (1, 2): 12,
    (2, 3): 13,
    (3, 2): 14,
    (2, 2): 15,
}
COLUMNS = len(PLACE)
STEPS = COLUMNS // 2
ARRIVE = {
    0: [(1, 0), (3, 0), (0, 1), (0, 3)],
    1: [(1, 1), (2, 0)],
    2: [(3, 3), (3, 1), (1, 3)],
    3: [(0, 2)],
    4: [(2, 1), (2, 3), (1, 2)],
    5: [(3, 2)],
    6: [(2, 2)],
}


def layer_kernel(
    query,
    key,
    value,
    residual,
    weight,
    gate_table,
    span_of_shard,
    noise_level,
    visible,
    out,
    kv,
    q_in,
    q_rows,
    top,
    acc,
    att_out,
    att,
    w_here,
    res_here,
    gate_here,
    part_out,
    part_in,
    part_keep,
    cross_out,
    cross_in,
    mask,
    local_sem,
    k_send,
    k_recv,
    v_send,
    v_recv,
    q_send,
    q_recv,
    g_send,
    g_recv,
    s_send,
    s_recv,
    a_send,
    a_recv,
    p_send,
    p_recv,
    c_send,
    c_recv,
):
    ctx = lax.axis_index("ctx")
    head = lax.axis_index("head")
    y_hi, x, z = ctx // 16, (ctx // 4) % 4, ctx % 4
    y_lo, core = head // 2, head % 2
    y = y_hi * 2 + y_lo
    other = 1 - core

    def device(y_at, x_at, z_at, core_at):
        return ((y_at // 2) * 16 + x_at * 4 + z_at, (y_at % 2) * 2 + core_at)

    def in_column(step, core_at):
        return device((y + step) % 4, x, z, core_at)

    sibling = in_column(0, other)

    def along(axis, step):
        on_x = (1 - core) if axis == 0 else core
        return device(y, (x + on_x * (step + 4)) % 4, (z + (1 - on_x) * (step + 4)) % 4, core)

    def place(first, second):
        a, b = PLACE[(first, second)], PLACE[(second, first)]
        return a if a == b else a + core * (b - a)

    def remote(src, dst, send, recv, to):
        return pltpu.make_async_remote_copy(
            src_ref=src, dst_ref=dst, send_sem=send, recv_sem=recv, device_id=to, device_id_type=MESH
        )

    local = [
        pltpu.make_async_copy(weight, w_here, local_sem.at[0]),
        pltpu.make_async_copy(residual, res_here, local_sem.at[1]),
        pltpu.make_async_copy(gate_table, gate_here, local_sem.at[2]),
    ]

    barrier = pltpu.get_barrier_semaphore()
    peers = [in_column(1, core), in_column(2, core), in_column(3, core)]
    peers += [sibling, in_column(2, other)]
    peers += [along(0, 1), along(0, -1), along(1, 1), along(1, -1)]
    for peer in peers:
        pl.semaphore_signal(barrier, inc=1, device_id=peer, device_id_type=MESH)
    pl.semaphore_wait(barrier, len(peers))

    key_rows = pl.ds(pl.multiple_of(y_lo * BLOCK, BLOCK), BLOCK)

    def key_copy(step, which):
        chip = (y + step) % 4
        group = (chip % 2) * 2 + chip // 2
        src = (key, value)[which].at[:, pl.ds(pl.multiple_of(group * HD, HD), HD)]
        dst = kv.at[0, core, y_hi, which, key_rows]
        send, recv = ((k_send, k_recv), (v_send, v_recv))[which]
        if step == 0:
            return pltpu.make_async_copy(src, dst, recv.at[0])
        return remote(src, dst, send.at[step], recv.at[step], in_column(step, core))

    def query_copy(step):
        chip = (y + step) % 4
        group = (chip % 2) * 2 + chip // 2
        src = query.at[:, pl.ds(pl.multiple_of(group * WIDTH, WIDTH), WIDTH)]
        block = {0: 3, 1: 1 - core, 2: 2, 3: core}[step]
        dst = q_in.at[block]
        if step == 0:
            return pltpu.make_async_copy(src, dst, q_recv.at[0])
        return remote(src, dst, q_send.at[step], q_recv.at[step], in_column(step, core))

    for step in (2, 1, 3, 0):
        for which in range(2):
            key_copy(step, which).start()
    for step in (1, 3, 2, 0):
        query_copy(step).start()
    for copy in local:
        copy.start()

    span_here = [span_of_shard[x * 4 + z], span_of_shard[16 + x * 4 + z]]
    for (dx, dz), at in PLACE.items():
        column = ((x + 4 - dx) % 4) * 4 + (z + 4 - dz) % 4
        for half in range(2):
            span = span_of_shard[half * 16 + column]
            for row in range(2):
                mask[row, at * 2 + half] = visible[span_here[row], span]

    top[...] = jnp.full(top.shape, NEG, jnp.float32)
    acc[...] = jnp.zeros(acc.shape, jnp.float32)

    def full_copy(first, second, axis, step):
        src = kv.at[place(first, second), core]
        there = ((first + step) % 4, second) if axis == 0 else (first, (second + step) % 4)
        at = place(*there)
        return remote(src, kv.at[at, core], g_send.at[at, 0], g_recv.at[at, 0], along(axis, step))

    def half_copy(first, second, axis, step):
        half = 0 if step == 1 else 1
        src = kv.at[place(first, second), core, half]
        there = ((first + step) % 4, second) if axis == 0 else (first, (second + step) % 4)
        at = place(*there)
        return remote(
            src, kv.at[at, core, half], g_send.at[at, half], g_recv.at[at, half], along(axis, step)
        )

    def side_copy(at):
        return remote(kv.at[at, core], kv.at[at, core], s_send.at[at], s_recv.at[at], sibling)

    def side_wait(at):
        remote(kv.at[at, other], kv.at[at, other], s_send.at[at], s_recv.at[at], sibling).wait_recv()

    def onward(first, second):
        copies = []
        if second == 0:
            if first == 0:
                copies += [full_copy(0, 0, 0, 1), full_copy(0, 0, 0, -1)]
            if first == 1:
                copies += [half_copy(1, 0, 0, 1)]
            if first == 3:
                copies += [half_copy(3, 0, 0, -1)]
            copies += [full_copy(first, 0, 1, 1), full_copy(first, 0, 1, -1)]
        elif second == 1:
            copies += [half_copy(first, 1, 1, 1)]
        elif second == 3:
            copies += [half_copy(first, 3, 1, -1)]
        return copies + [side_copy(place(first, second))]

    def arrive(first, second):
        at = place(first, second)
        if (second if second else first) == 2:
            for half in range(2):
                spot = kv.at[at, core, half]
                remote(spot, spot, g_send.at[at, half], g_recv.at[at, half], sibling).wait_recv()
        else:
            spot = kv.at[at, core]
            remote(spot, spot, g_send.at[at, 0], g_recv.at[at, 0], sibling).wait_recv()
        for copy in onward(first, second):
            copy.start()

    for step in range(4):
        for which in range(2):
            copy = key_copy(step, which)
            if step == 0:
                copy.wait()
            else:
                copy.wait_recv()
    for copy in onward(0, 0):
        copy.start()
    for offset in ARRIVE[0]:
        arrive(*offset)

    scale = math.log2(math.e) / math.sqrt(HD)

    def take_queries(block):
        for one in range(SHARE):
            rows = q_in[block, :, one * HD : (one + 1) * HD].astype(jnp.float32) * scale
            upper = rows.astype(jnp.bfloat16)
            lower = (rows - upper.astype(jnp.float32)).astype(jnp.bfloat16)
            spot = pl.ds(block * ROWS + one * BLOCK, BLOCK)
            q_rows[spot, :HD] = upper
            q_rows[spot, HD:] = lower

    def block_chip(block):
        step = [1 + core * 2, 3 - core * 2, 2, 0][block]
        return (y + step) % 4

    def attend(blocks, i):
        groups = [(2 * i + late, half) for late in range(2) for half in range(2)]
        spots = [(at, side, half) for at, half in groups for side in range(2)]
        keys = jnp.concatenate([kv[at, side, half, 0] for at, side, half in spots], axis=0)
        keys = jnp.concatenate([keys, keys], axis=1)
        values = jnp.concatenate([kv[at, side, half, 1] for at, side, half in spots], axis=0)
        values = jnp.concatenate([values, jnp.ones_like(values)], axis=1)
        scores = [
            lax.dot_general(
                q_rows[block * ROWS : (block + 1) * ROWS],
                keys,
                (((1,), (1,)), ((), ())),
                preferred_element_type=jnp.float32,
            )
            for block in blocks
        ]
        ready = []
        for block, score in zip(blocks, scores):
            rows = slice(block * ROWS, (block + 1) * ROWS)
            shard = block_chip(block) // 2
            seen = [mask[shard, at * 2 + half] > 0 for at, half in groups]
            parts = [score[:, n * 2 * HD : (n + 1) * 2 * HD] for n in range(len(groups))]
            best = None
            for part, ok in zip(parts, seen):
                most = jnp.where(ok, jnp.maximum(part[:, :HD], part[:, HD:]), NEG)
                best = most if best is None else jnp.maximum(best, most)
            old = top[rows]
            new = jnp.maximum(old, jnp.max(best, axis=1, keepdims=True))
            top[rows] = new
            weights = [
                jnp.exp2(part - jnp.where(ok, new, BIG)).astype(jnp.bfloat16)
                for part, ok in zip(parts, seen)
            ]
            ready.append((rows, jnp.concatenate(weights, axis=1), jnp.exp2(old - new)))
        for rows, weights, factor in ready:
            acc[rows] = acc[rows] * factor + jnp.dot(
                weights, values, preferred_element_type=jnp.float32
            )

    def far_copy(phase, block):
        src = att_out.at[block]
        dst = att.at[phase, pl.ds(pl.multiple_of(core * BLOCK, BLOCK), BLOCK)]
        return remote(
            src, dst, a_send.at[phase, 0], a_recv.at[phase, core], in_column(2, y_hi)
        )

    def near_copy(phase, block, stays):
        src = att_out.at[block]
        dst = att.at[phase, pl.ds(pl.multiple_of(core * BLOCK, BLOCK), BLOCK)]
        if stays:
            return pltpu.make_async_copy(src, dst, a_recv.at[phase, core])
        return remote(src, dst, a_send.at[phase, 1], a_recv.at[phase, core], sibling)

    def send_attended(phase):
        for block in (2 * phase, 2 * phase + 1):
            rows = slice(block * ROWS, (block + 1) * ROWS)
            attended = (acc[rows, :HD] / acc[rows, HD:]).astype(jnp.bfloat16)
            for one in range(SHARE):
                att_out[block, :, one * HD : (one + 1) * HD] = attended[
                    one * BLOCK : (one + 1) * BLOCK
                ]
        far_copy(phase, 2 * phase).start()

        @pl.when(core == y_hi)
        def _():
            near_copy(phase, 2 * phase + 1, True).start()

        @pl.when(core != y_hi)
        def _():
            near_copy(phase, 2 * phase + 1, False).start()

    def part_copy(phase, n):
        return remote(
            part_out.at[phase, n],
            part_in.at[phase, n],
            p_send.at[phase, n],
            p_recv.at[phase, n],
            sibling,
        )

    def cross_copy(n):
        return remote(
            cross_out.at[n],
            cross_in.at[n],
            c_send.at[n],
            c_recv.at[n],
            in_column(3 - 2 * core, core),
        )

    def project(phase):
        for side in range(2):
            spot = att.at[phase, side * BLOCK : (side + 1) * BLOCK]
            remote(spot, spot, a_send.at[phase, 0], a_recv.at[phase, side], sibling).wait_recv()
        rows = att[phase]
        for n in range(CHUNKS):
            part = jnp.dot(
                rows,
                w_here[:, n * CHUNK : (n + 1) * CHUNK],
                preferred_element_type=jnp.float32,
            )
            first, second = part[:BLOCK], part[BLOCK:]
            part_out[phase, n] = jnp.where(core == 0, second, first).astype(jnp.bfloat16)
            part_copy(phase, n).start()
            part_keep[n] = jnp.where(core == 0, first, second)

    def cross_send():
        for n in range(CHUNKS):
            part_copy(0, n).wait_recv()
            total = part_keep[n] + part_in[0, n].astype(jnp.float32)
            cross_out[n] = total.astype(jnp.bfloat16)
            cross_copy(n).start()

    query_copy(1).wait_recv()
    query_copy(3).wait_recv()
    take_queries(0)
    take_queries(1)

    def early(i, carry):
        for at in ARRIVE:
            if at:

                @pl.when(i == at)
                def _(at=at):
                    for offset in ARRIVE[at]:
                        arrive(*offset)

        @pl.when(i > 0)
        def _():
            side_wait(2 * i)

        side_wait(2 * i + 1)
        attend((0, 1), i)
        return carry

    side_wait(0)
    lax.fori_loop(0, STEPS, early, 0)
    send_attended(0)
    local[0].wait()

    query_copy(0).wait()
    query_copy(2).wait_recv()
    take_queries(2)
    take_queries(3)

    def late(i, carry):
        attend((2, 3), i)

        @pl.when(i == 1)
        def _():
            project(0)

        @pl.when(i == 3)
        def _():
            cross_send()

        return carry

    lax.fori_loop(0, STEPS, late, 0)
    send_attended(1)
    local[1].wait()
    local[2].wait()
    level = noise_level[span_here[0] * (1 - y_hi) + span_here[1] * y_hi]
    project(1)
    for n in range(CHUNKS):
        columns = slice(n * CHUNK, (n + 1) * CHUNK)
        gate = jnp.zeros((1, CHUNK), jnp.float32)
        for at in range(gate_here.shape[0]):
            gate = jnp.where(level == at, gate_here[at : at + 1, columns], gate)
        part_copy(1, n).wait_recv()
        cross_copy(n).wait_recv()
        total = part_keep[n] + part_in[1, n].astype(jnp.float32) + cross_in[n].astype(jnp.float32)
        out[:, columns] = (res_here[:, columns].astype(jnp.float32) + gate * total).astype(
            jnp.bfloat16
        )

    for step in (1, 2, 3):
        key_copy(step, 0).wait_send()
        key_copy(step, 1).wait_send()
        query_copy(step).wait_send()
    for first in range(4):
        for second in range(4):
            for copy in onward(first, second):
                copy.wait_send()
    for phase in range(2):
        far_copy(phase, 2 * phase).wait_send()

        @pl.when(core != y_hi)
        def _(phase=phase):
            near_copy(phase, 2 * phase + 1, False).wait_send()

        for n in range(CHUNKS):
            part_copy(phase, n).wait_send()
    for n in range(CHUNKS):
        cross_copy(n).wait_send()


def on_device(*arrays):
    anywhere = pl.BlockSpec(memory_space=pl.ANY)
    scalars = pl.BlockSpec(memory_space=pltpu.SMEM)
    bf16, f32 = jnp.bfloat16, jnp.float32
    dma = pltpu.SemaphoreType.DMA
    return pl.pallas_call(
        layer_kernel,
        out_shape=jax.ShapeDtypeStruct((BLOCK, D), bf16),
        in_specs=[anywhere] * 6 + [scalars] * 3,
        out_specs=pl.BlockSpec(memory_space=pltpu.VMEM),
        scratch_shapes=[
            pltpu.VMEM((COLUMNS, 2, 2, 2, HD, HD), bf16),
            pltpu.VMEM((4, BLOCK, WIDTH), bf16),
            pltpu.VMEM((4 * ROWS, 2 * HD), bf16),
            pltpu.VMEM((4 * ROWS, 1), f32),
            pltpu.VMEM((4 * ROWS, 2 * HD), f32),
            pltpu.VMEM((4, BLOCK, WIDTH), bf16),
            pltpu.VMEM((2, 2 * BLOCK, WIDTH), bf16),
            pltpu.VMEM((WIDTH, D), bf16),
            pltpu.VMEM((BLOCK, D), bf16),
            pltpu.VMEM((4, D), f32),
            pltpu.VMEM((2, CHUNKS, BLOCK, CHUNK), bf16),
            pltpu.VMEM((2, CHUNKS, BLOCK, CHUNK), bf16),
            pltpu.VMEM((CHUNKS, BLOCK, CHUNK), f32),
            pltpu.VMEM((CHUNKS, BLOCK, CHUNK), bf16),
            pltpu.VMEM((CHUNKS, BLOCK, CHUNK), bf16),
            pltpu.SMEM((2, 2 * COLUMNS), jnp.int32),
            dma((3,)),
            dma((4,)),
            dma((4,)),
            dma((4,)),
            dma((4,)),
            dma((4,)),
            dma((4,)),
            dma((COLUMNS, 2)),
            dma((COLUMNS, 2)),
            dma((COLUMNS,)),
            dma((COLUMNS,)),
            dma((2, 2)),
            dma((2, 2)),
            dma((2, CHUNKS)),
            dma((2, CHUNKS)),
            dma((CHUNKS,)),
            dma((CHUNKS,)),
        ],
        compiler_params=pltpu.CompilerParams(
            collective_id=0, has_side_effects=True, vmem_limit_bytes=58 * 2**20
        ),
        name="span_attention_layer",
    )(*arrays)


def solution(mesh):
    tokens = P(("ctx", "head"), None)
    placed = (tokens, tokens, tokens, tokens, P("head", None), P(), P(), P(), P())
    return jax.shard_map(
        on_device, mesh=mesh, in_specs=placed, out_specs=tokens, check_vma=False
    )
```

time: 303 us -> 65.1 us (0.21)
  waiting for transfers between devices: 158 us -> 0 us
  matrix products: 82.5 us -> 0 us
  Pallas kernels: 0 us -> 62.6 us
  other arithmetic: 19.6 us -> 0 us
  blocking collectives: 14.9 us -> 0 us
  between operations: 13.2 us -> 0.01 us
  local copies, waits for them, and re-layouts: 8.87 us -> 2.06 us
  starting transfers between devices: 4.34 us -> 0 us
    all_gather x2 -> x0, waiting for transfers between devices: 122 us -> none  [the longest x1 70.9 us: on_device(): lax.all_gather(local_v, 'ctx', axis=0, tiled=True)]
    dot_general x26 -> x0, matrix products: 82.5 us -> none  [the longest x8 37.8 us: block_update(): jnp.einsum('qagd,kad->agqk', queries, keys, preferred_element_type=jnp.fl...]
    pallas_call x0 -> x1, Pallas kernels: none -> 62.6 us  [on_device(): pl.pallas_call(layer_kernel, out_shape=jax.ShapeDtypeStruct((BLOCK, D), b...]
    reduce_scatter x1 -> x0, waiting for transfers between devices: 33.3 us -> none  [on_device(): lax.psum_scatter(jnp.dot(attended, out_weight, preferred_element_type=jnp...]
    reduce_sum x12 -> x0, other arithmetic: 15.8 us -> none  [the longest x8 12.1 us: block_update(): l_new = l_old * factor + jnp.sum(weights, axis=3)]
    all_to_all x2 -> x0, blocking collectives: 14.9 us -> none  [the longest x1 7.71 us: on_device(): lax.all_to_all(key, 'head', split_axis=1, concat_axis=0, tiled=True)]
    while x25 -> x0, local copies, waits for them, and re-layouts: 4.79 us -> none
    all_to_all x1 -> x0, starting transfers between devices: 4.29 us -> none  [on_device(): lax.all_to_all(query, 'head', split_axis=1, concat_axis=0, tiled=True)]
  transfers between devices with their start and end apart: 4 -> 0, of which waited for: 4 -> 0; matrix products, arithmetic and copies ran while one was open for 3% -> 0% of each run, Pallas kernels for 0% -> 0%
where the time goes in v1:
time: 65.1 us; the launch traced here: 64.7 us
  Pallas kernels  62.6 us (96%)
  local copies, waits for them, and re-layouts  2.06 us (3%)
    pallas_call x1, Pallas kernels, on_device(): pl.pallas_call(layer_kernel, out_shape=jax.ShapeDtypeStruct((BLOCK, D), b...  62.6 us
    unnamed x1, local copies, waits for them, and re-layouts  2.06 us

profile of v1, /device:TPU:1, one launch (start us, length us, event | category | flops | bytes accessed | tf_op | source)
XLA Modules:
  0.0 64.7 jit_solution(11657412033427653285)
XLA Ops:
  0.0 62.6 %span_attention_layer.1 = bf16[64,6144]{1,0:T(8,128)(2,1)} custom-call(bf16[64,3072]{1,0:T(8,128)(2,1)} %query.1, bf16[64,512]{1,0:T(8,128)(2,1)} %key.1, bf16[64,512]{1,0:T(8,128)(2,1)} %value.1, bf16[64,6144]{1,0:T(8,128)(2,1)} %residual.1, bf16[768,6144]{1,0:T(8,128)(2,1)} %weight.1, f32[4,6144]{1,0:T(4,128)} %gate_table.1, s32[32]{0:T(128)} %span_of_shard.1, ...), custom_call_target="tpu_custom_call" | custom-call | tf_op jit(solution)/shard_map/span_attention_layer/pallas_call | solution.py:460
  62.6 2.1 %copy.11 = bf16[64,6144]{1,0:T(8,128)(2,1)} copy(bf16[64,6144]{1,0:T(8,128)(2,1)} %span_attention_layer.1) | data formatting | bytes 1572864

commit v2 on v1

v2 whole, which is shorter than its diff:
```python
import math

import jax
import jax.numpy as jnp
from jax import lax
from jax.experimental import pallas as pl
from jax.experimental.pallas import tpu as pltpu
from jax.sharding import PartitionSpec as P

HD = 128
KV_HEADS = 4
SHARE = 6
WIDTH = SHARE * HD
BLOCK = 64
ROWS = SHARE * BLOCK
D = 6144
CHUNKS = 6
CHUNK = D // CHUNKS
RING = 4
NEG = -1e30
BIG = 1e30
MESH = pl.DeviceIdType.MESH

PLACE = {
    (0, 0): 0,
    (1, 0): 1,
    (0, 1): 2,
    (3, 0): 3,
    (0, 3): 4,
    (1, 1): 5,
    (3, 3): 6,
    (3, 1): 7,
    (1, 3): 8,
    (2, 0): 9,
    (0, 2): 10,
    (2, 1): 11,
    (1, 2): 12,
    (2, 3): 13,
    (3, 2): 14,
    (2, 2): 15,
}
COLUMNS = len(PLACE)
STEPS = COLUMNS // 2
FILL = {1: (0, 1)}
AHEAD = 1
LEFT = STEPS - AHEAD
LAG = 4
FIRST = [(1, 0), (3, 0), (0, 1), (0, 3)]
ARRIVE = {
    1: [(1, 1), (3, 3), (3, 1), (1, 3), (0, 2)],
    3: [(2, 1), (2, 3)],
    5: [(2, 2)],
}
MIDDLE = {
    0: [(2, 0)],
    3: [(1, 2), (3, 2)],
}


def layer_kernel(
    query,
    key,
    value,
    residual,
    weight,
    gate_table,
    span_of_shard,
    noise_level,
    visible,
    out,
    kv,
    q_in,
    q_rows,
    top,
    acc,
    score_a,
    score_b,
    weight_a,
    weight_b,
    factor_a,
    factor_b,
    score_c,
    score_d,
    weight_c,
    weight_d,
    factor_c,
    factor_d,
    att_out,
    att,
    w_here,
    res_here,
    gate_here,
    part_out,
    part_in,
    part_keep,
    cross_out,
    cross_in,
    mask,
    q_own,
    k_own,
    v_own,
    local_sem,
    k_send,
    k_recv,
    v_send,
    v_recv,
    q_send,
    q_recv,
    g_send,
    g_recv,
    s_send,
    s_recv,
    a_send,
    a_recv,
    p_send,
    p_recv,
    c_send,
    c_recv,
    o_sem,
):
    ctx = lax.axis_index("ctx")
    head = lax.axis_index("head")
    y_hi, x, z = ctx // 16, (ctx // 4) % 4, ctx % 4
    y_lo, core = head // 2, head % 2
    y = y_hi * 2 + y_lo
    other = 1 - core

    def device(y_at, x_at, z_at, core_at):
        return ((y_at // 2) * 16 + x_at * 4 + z_at, (y_at % 2) * 2 + core_at)

    def in_column(step, core_at):
        return device((y + step) % 4, x, z, core_at)

    sibling = in_column(0, other)

    def along(axis, step):
        on_x = (1 - core) if axis == 0 else core
        return device(y, (x + on_x * (step + 4)) % 4, (z + (1 - on_x) * (step + 4)) % 4, core)

    def place(first, second):
        a, b = PLACE[(first, second)], PLACE[(second, first)]
        return a if a == b else a + core * (b - a)

    def remote(src, dst, send, recv, to):
        return pltpu.make_async_remote_copy(
            src_ref=src, dst_ref=dst, send_sem=send, recv_sem=recv, device_id=to, device_id_type=MESH
        )

    local = [
        pltpu.make_async_copy(weight, w_here, local_sem.at[0]),
        pltpu.make_async_copy(residual, res_here, local_sem.at[1]),
        pltpu.make_async_copy(gate_table, gate_here, local_sem.at[2]),
    ]

    own = [
        pltpu.make_async_copy(key, k_own, local_sem.at[3]),
        pltpu.make_async_copy(value, v_own, local_sem.at[4]),
        pltpu.make_async_copy(query, q_own, local_sem.at[5]),
    ]
    for copy in own:
        copy.start()

    barrier = pltpu.get_barrier_semaphore()
    peers = [in_column(1, core), in_column(2, core), in_column(3, core)]
    peers += [sibling, in_column(2, other)]
    peers += [along(0, 1), along(0, -1), along(1, 1), along(1, -1)]
    for peer in peers:
        pl.semaphore_signal(barrier, inc=1, device_id=peer, device_id_type=MESH)
    top[...] = jnp.full(top.shape, NEG, jnp.float32)
    acc[...] = jnp.zeros(acc.shape, jnp.float32)
    for copy in own:
        copy.wait()
    pl.semaphore_wait(barrier, len(peers))

    key_rows = pl.ds(pl.multiple_of(y_lo * BLOCK, BLOCK), BLOCK)

    def key_copy(step, which):
        chip = (y + step) % 4
        group = (chip % 2) * 2 + chip // 2
        src = (k_own, v_own)[which].at[:, pl.ds(pl.multiple_of(group * HD, HD), HD)]
        dst = kv.at[0, core, y_hi, which, key_rows]
        send, recv = ((k_send, k_recv), (v_send, v_recv))[which]
        if step == 0:
            return pltpu.make_async_copy(src, dst, recv.at[0])
        return remote(src, dst, send.at[step], recv.at[step], in_column(step, core))

    def query_copy(step):
        chip = (y + step) % 4
        group = (chip % 2) * 2 + chip // 2
        src = q_own.at[:, pl.ds(pl.multiple_of(group * WIDTH, WIDTH), WIDTH)]
        block = {0: 3, 1: 1 - core, 2: 2, 3: core}[step]
        dst = q_in.at[block]
        if step == 0:
            return pltpu.make_async_copy(src, dst, q_recv.at[0])
        return remote(src, dst, q_send.at[step], q_recv.at[step], in_column(step, core))

    for step in (2, 1, 3, 0):
        for which in range(2):
            key_copy(step, which).start()
    for step in (1, 3, 0):
        query_copy(step).start()
    for copy in local:
        copy.start()

    span_here = [span_of_shard[x * 4 + z], span_of_shard[16 + x * 4 + z]]
    for (dx, dz), at in PLACE.items():
        column = ((x + 4 - dx) % 4) * 4 + (z + 4 - dz) % 4
        for half in range(2):
            span = span_of_shard[half * 16 + column]
            for row in range(2):
                mask[row, at * 2 + half] = visible[span_here[row], span]

    def ring_copy(first, second, axis, step, half):
        there = ((first + step) % 4, second) if axis == 0 else (first, (second + step) % 4)
        at = place(*there)
        if half is None:
            src, dst, n = kv.at[place(first, second), core], kv.at[at, core], 0
        else:
            src, dst, n = kv.at[place(first, second), core, half], kv.at[at, core, half], half
        return remote(src, dst, g_send.at[at, n], g_recv.at[at, n], along(axis, step))

    def side_copy(at):
        return remote(kv.at[at, core], kv.at[at, core], s_send.at[at], s_recv.at[at], sibling)

    def side_wait(at):
        remote(kv.at[at, other], kv.at[at, other], s_send.at[at], s_recv.at[at], sibling).wait_recv()

    def onward(first, second):
        ways = []
        if second == 0:
            if first == 0:
                ways += [(0, 1, None), (0, -1, None)]
            if first == 1:
                ways += [(0, 1, 0)]
            if first == 3:
                ways += [(0, -1, 1)]
            ways += [(1, 1, None), (1, -1, None)]
        elif second == 1:
            ways += [(1, 1, 0)]
        elif second == 3:
            ways += [(1, -1, 1)]
        return [ring_copy(first, second, *way) for way in ways]

    def arrive(first, second):
        at = place(first, second)
        if (second if second else first) == 2:
            for half in range(2):
                spot = kv.at[at, core, half]
                remote(spot, spot, g_send.at[at, half], g_recv.at[at, half], sibling).wait_recv()
        else:
            spot = kv.at[at, core]
            remote(spot, spot, g_send.at[at, 0], g_recv.at[at, 0], sibling).wait_recv()
        for copy in onward(first, second):
            copy.start()
        side_copy(at).start()

    for step in range(4):
        for which in range(2):
            copy = key_copy(step, which)
            if step == 0:
                copy.wait()
            else:
                copy.wait_recv()
    for copy in onward(0, 0):
        copy.start()
    side_copy(0).start()
    weight_a[...] = jnp.zeros(weight_a.shape, jnp.bfloat16)
    weight_b[...] = jnp.zeros(weight_b.shape, jnp.bfloat16)
    factor_a[...] = jnp.ones(factor_a.shape, jnp.float32)
    factor_b[...] = jnp.ones(factor_b.shape, jnp.float32)
    for offset in FIRST:
        arrive(*offset)

    scale = math.log2(math.e) / math.sqrt(HD)

    def take_queries(block):
        for one in range(SHARE):
            rows = q_in[block, :, one * HD : (one + 1) * HD].astype(jnp.float32) * scale
            upper = rows.astype(jnp.bfloat16)
            lower = (rows - upper.astype(jnp.float32)).astype(jnp.bfloat16)
            spot = pl.ds(block * ROWS + one * BLOCK, BLOCK)
            q_rows[spot, :HD] = upper
            q_rows[spot, HD:] = lower

    def rows_of(block):
        if isinstance(block, int):
            return pl.ds(block * ROWS, ROWS)
        return pl.ds(pl.multiple_of(block * ROWS, ROWS), ROWS)

    def groups_of(pair):
        return [(2 * pair + late, half) for late in range(2) for half in range(2)]

    def both_sides(pair, which):
        return jnp.concatenate(
            [kv[at, side, half, which] for at, half in groups_of(pair) for side in range(2)], axis=0
        )

    scores = (score_a, score_b, score_c, score_d)
    weights = (weight_a, weight_b, weight_c, weight_d)
    factors = (factor_a, factor_b, factor_c, factor_d)

    def score(block, pair, slot):
        keys = both_sides(pair, 0)
        keys = jnp.concatenate([keys, keys], axis=1)
        scores[slot][...] = lax.dot_general(
            q_rows[rows_of(block)],
            keys,
            (((1,), (1,)), ((), ())),
            preferred_element_type=jnp.float32,
        )

    def weigh(block, shard, pair, slot):
        rows = rows_of(block)
        groups = groups_of(pair)
        seen = [mask[shard, at * 2 + half] > 0 for at, half in groups]
        parts = [scores[slot][:, n * 2 * HD : (n + 1) * 2 * HD] for n in range(len(groups))]
        best = None
        for part, ok in zip(parts, seen):
            most = jnp.where(ok, jnp.maximum(part[:, :HD], part[:, HD:]), NEG)
            best = most if best is None else jnp.maximum(best, most)
        old = top[rows]
        new = jnp.maximum(old, jnp.max(best, axis=1, keepdims=True))
        top[rows] = new
        for n, (part, ok) in enumerate(zip(parts, seen)):
            weights[slot][:, n * 2 * HD : (n + 1) * 2 * HD] = jnp.exp2(
                part - jnp.where(ok, new, BIG)
            ).astype(jnp.bfloat16)
        factors[slot][...] = jnp.exp2(old - new)

    def gather(block, pair, slot):
        rows = rows_of(block)
        values = both_sides(pair, 1)
        values = jnp.concatenate([values, jnp.ones_like(values)], axis=1)
        acc[rows] = acc[rows] * factors[slot][...] + jnp.dot(
            weights[slot][...], values, preferred_element_type=jnp.float32
        )

    def shard_at(step):
        return ((y + step) % 4) // 2

    def far_copy(phase, block):
        src = att_out.at[block]
        dst = att.at[phase, pl.ds(pl.multiple_of(core * BLOCK, BLOCK), BLOCK)]
        return remote(
            src, dst, a_send.at[phase, 0], a_recv.at[phase, core], in_column(2, y_hi)
        )

    def near_copy(phase, block, stays):
        src = att_out.at[block]
        dst = att.at[phase, pl.ds(pl.multiple_of(core * BLOCK, BLOCK), BLOCK)]
        if stays:
            return pltpu.make_async_copy(src, dst, a_recv.at[phase, core])
        return remote(src, dst, a_send.at[phase, 1], a_recv.at[phase, core], sibling)

    def normalise(block):
        rows = rows_of(block)
        attended = (acc[rows, :HD] / acc[rows, HD:]).astype(jnp.bfloat16)
        for one in range(SHARE):
            att_out[block, :, one * HD : (one + 1) * HD] = attended[one * BLOCK : (one + 1) * BLOCK]

    def send_far(phase):
        normalise(2 * phase)
        far_copy(phase, 2 * phase).start()

    def send_near(phase):
        normalise(2 * phase + 1)

        @pl.when(core == y_hi)
        def _():
            near_copy(phase, 2 * phase + 1, True).start()

        @pl.when(core != y_hi)
        def _():
            near_copy(phase, 2 * phase + 1, False).start()

    def part_copy(phase, n):
        return remote(
            part_out.at[phase, n],
            part_in.at[phase, n],
            p_send.at[phase, n],
            p_recv.at[phase, n],
            sibling,
        )

    def cross_copy(n):
        return remote(
            cross_out.at[n],
            cross_in.at[n],
            c_send.at[n],
            c_recv.at[n],
            in_column(3 - 2 * core, core),
        )

    def cross_send(n):
        part_copy(0, n).wait_recv()
        total = part_keep[n] + part_in[0, n].astype(jnp.float32)
        cross_out[n] = total.astype(jnp.bfloat16)
        cross_copy(n).start()

    def out_copy(n):
        columns = pl.ds(n * CHUNK, CHUNK)
        return pltpu.make_async_copy(res_here.at[:, columns], out.at[:, columns], o_sem.at[n])

    level = noise_level[span_here[0] * (1 - y_hi) + span_here[1] * y_hi]

    def finish(n):
        columns = slice(n * CHUNK, (n + 1) * CHUNK)
        gate = jnp.zeros((1, CHUNK), jnp.float32)
        for at in range(gate_here.shape[0]):
            gate = jnp.where(level == at, gate_here[at : at + 1, columns], gate)
        part_copy(1, n).wait_recv()
        cross_copy(n).wait_recv()
        total = part_keep[n] + part_in[1, n].astype(jnp.float32) + cross_in[n].astype(jnp.float32)
        res_here[:, columns] = (res_here[:, columns].astype(jnp.float32) + gate * total).astype(
            jnp.bfloat16
        )
        out_copy(n).start()

    def project(phase, use):
        for side in range(2):
            spot = att.at[phase, side * BLOCK : (side + 1) * BLOCK]
            remote(spot, spot, a_send.at[phase, 0], a_recv.at[phase, side], sibling).wait_recv()
        rows = att[phase]
        for n in range(CHUNKS + LAG):
            if n < CHUNKS:
                part = jnp.dot(
                    rows,
                    w_here[:, n * CHUNK : (n + 1) * CHUNK],
                    preferred_element_type=jnp.float32,
                )
                first, second = part[:BLOCK], part[BLOCK:]
                part_out[phase, n] = jnp.where(core == 0, second, first).astype(jnp.bfloat16)
                part_copy(phase, n).start()
                part_keep[n] = jnp.where(core == 0, first, second)
            if n >= LAG:
                use(n - LAG)

    query_copy(1).wait_recv()
    query_copy(3).wait_recv()
    query_copy(2).start()
    take_queries(0)
    take_queries(1)
    side_wait(0)
    side_wait(1)
    score(0, 0, 0)
    last = STEPS - 1

    def ahead(pair, carry):
        for block in (2, 3):
            score(block, pair, block)
        for block in (2, 3):
            weigh(block, shard_at(6 - 2 * block), pair, block)
        for block in (2, 3):
            gather(block, pair, block)
        return carry

    def early(i, carry):
        @pl.when(i == 1)
        def _():
            query_copy(0).wait()
            query_copy(2).wait_recv()
            take_queries(2)
            take_queries(3)

        for at, (low, high) in FILL.items():

            @pl.when(i == at)
            def _(low=low, high=high):
                lax.fori_loop(low, high, ahead, 0)

        for at in ARRIVE:

            @pl.when(i == at)
            def _(at=at):
                for offset in ARRIVE[at]:
                    arrive(*offset)

        gather(1, jnp.maximum(i - 1, 0), 1)
        score(1, i, 1)
        weigh(0, shard_at(1 + 2 * core), i, 0)
        for at in MIDDLE:

            @pl.when(i == at)
            def _(at=at):
                for offset in MIDDLE[at]:
                    arrive(*offset)

        @pl.when(i < last)
        def _():
            side_wait(2 * i + 2)
            side_wait(2 * i + 3)

        gather(0, i, 0)
        score(jnp.where(i == last, 2, 0), jnp.where(i == last, AHEAD, i + 1), 0)
        weigh(1, shard_at(3 - 2 * core), i, 1)
        return carry

    lax.fori_loop(0, STEPS, early, 0)
    send_far(0)
    local[0].wait()

    def block_of(n):
        return 2 + n // LEFT

    def pair_of(n):
        return AHEAD + n % LEFT

    def late(i, carry):
        n = 2 * i
        gather(
            jnp.where(i == 0, 1, block_of(jnp.maximum(n - 1, 0))),
            jnp.where(i == 0, last, pair_of(jnp.maximum(n - 1, 0))),
            1,
        )
        score(block_of(n + 1), pair_of(n + 1), 1)
        weigh(block_of(n), shard_at(6 - 2 * block_of(n)), pair_of(n), 0)
        gather(block_of(n), pair_of(n), 0)
        score(jnp.minimum(block_of(n + 2), 3), pair_of(n + 2), 0)
        weigh(block_of(n + 1), shard_at(6 - 2 * block_of(n + 1)), pair_of(n + 1), 1)

        @pl.when(i == 0)
        def _():
            send_near(0)

        @pl.when(i == LEFT // 2)
        def _():
            send_far(1)
            project(0, cross_send)

        return carry

    lax.fori_loop(0, LEFT, late, 0)
    gather(3, last, 1)
    send_near(1)
    local[1].wait()
    local[2].wait()
    project(1, finish)
    for n in range(CHUNKS):
        out_copy(n).wait()

    for step in (1, 2, 3):
        key_copy(step, 0).wait_send()
        key_copy(step, 1).wait_send()
        query_copy(step).wait_send()
    for first in range(4):
        for second in range(4):
            for copy in onward(first, second):
                copy.wait_send()
            side_copy(place(first, second)).wait_send()
    for phase in range(2):
        far_copy(phase, 2 * phase).wait_send()

        @pl.when(core != y_hi)
        def _(phase=phase):
            near_copy(phase, 2 * phase + 1, False).wait_send()

        for n in range(CHUNKS):
            part_copy(phase, n).wait_send()
    for n in range(CHUNKS):
        cross_copy(n).wait_send()


def on_device(*arrays):
    anywhere = pl.BlockSpec(memory_space=pl.ANY)
    scalars = pl.BlockSpec(memory_space=pltpu.SMEM)
    bf16, f32 = jnp.bfloat16, jnp.float32
    dma = pltpu.SemaphoreType.DMA
    return pl.pallas_call(
        layer_kernel,
        out_shape=jax.ShapeDtypeStruct((BLOCK, D), bf16),
        in_specs=[anywhere] * 6 + [scalars] * 3,
        out_specs=anywhere,
        scratch_shapes=[
            pltpu.VMEM((COLUMNS, 2, 2, 2, HD, HD), bf16),
            pltpu.VMEM((4, BLOCK, WIDTH), bf16),
            pltpu.VMEM((4 * ROWS, 2 * HD), bf16),
            pltpu.VMEM((4 * ROWS, 1), f32),
            pltpu.VMEM((4 * ROWS, 2 * HD), f32),
            pltpu.VMEM((ROWS, 8 * HD), f32),
            pltpu.VMEM((ROWS, 8 * HD), f32),
            pltpu.VMEM((ROWS, 8 * HD), bf16),
            pltpu.VMEM((ROWS, 8 * HD), bf16),
            pltpu.VMEM((ROWS, 1), f32),
            pltpu.VMEM((ROWS, 1), f32),
            pltpu.VMEM((ROWS, 8 * HD), f32),
            pltpu.VMEM((ROWS, 8 * HD), f32),
            pltpu.VMEM((ROWS, 8 * HD), bf16),
            pltpu.VMEM((ROWS, 8 * HD), bf16),
            pltpu.VMEM((ROWS, 1), f32),
            pltpu.VMEM((ROWS, 1), f32),
            pltpu.VMEM((4, BLOCK, WIDTH), bf16),
            pltpu.VMEM((2, 2 * BLOCK, WIDTH), bf16),
            pltpu.VMEM((WIDTH, D), bf16),
            pltpu.VMEM((BLOCK, D), bf16),
            pltpu.VMEM((4, D), f32),
            pltpu.VMEM((2, CHUNKS, BLOCK, CHUNK), bf16),
            pltpu.VMEM((2, CHUNKS, BLOCK, CHUNK), bf16),
            pltpu.VMEM((CHUNKS, BLOCK, CHUNK), f32),
            pltpu.VMEM((CHUNKS, BLOCK, CHUNK), bf16),
            pltpu.VMEM((CHUNKS, BLOCK, CHUNK), bf16),
            pltpu.SMEM((2, 2 * COLUMNS), jnp.int32),
            pltpu.VMEM((BLOCK, KV_HEADS * WIDTH), bf16),
            pltpu.VMEM((BLOCK, KV_HEADS * HD), bf16),
            pltpu.VMEM((BLOCK, KV_HEADS * HD), bf16),
            dma((6,)),
            dma((4,)),
            dma((4,)),
            dma((4,)),
            dma((4,)),
            dma((4,)),
            dma((4,)),
            dma((COLUMNS, 2)),
            dma((COLUMNS, 2)),
            dma((COLUMNS,)),
            dma((COLUMNS,)),
            dma((2, 2)),
            dma((2, 2)),
            dma((2, CHUNKS)),
            dma((2, CHUNKS)),
            dma((CHUNKS,)),
            dma((CHUNKS,)),
            dma((CHUNKS,)),
        ],
        compiler_params=pltpu.CompilerParams(
            collective_id=0, has_side_effects=True, vmem_limit_bytes=58 * 2**20
        ),
        name="span_attention_layer",
    )(*arrays)


def solution(mesh):
    tokens = P(("ctx", "head"), None)
    placed = (tokens, tokens, tokens, tokens, P("head", None), P(), P(), P(), P())
    return jax.shard_map(
        on_device, mesh=mesh, in_specs=placed, out_specs=tokens, check_vma=False
    )
```

time: 65.1 us -> 57 us (0.88)
  Pallas kernels: 62.6 us -> 54.7 us
    pallas_call x1, Pallas kernels: 62.6 us -> 54.7 us  [on_device(): pl.pallas_call(layer_kernel, out_shape=jax.ShapeDtypeStruct((BLOCK, D), b...]
where the time goes in v2:
time: 57 us; the launch traced here: 56.8 us
  Pallas kernels  54.7 us (96%)
  local copies, waits for them, and re-layouts  2.06 us (4%)
    pallas_call x1, Pallas kernels, on_device(): pl.pallas_call(layer_kernel, out_shape=jax.ShapeDtypeStruct((BLOCK, D), b...  54.7 us
    unnamed x1, local copies, waits for them, and re-layouts  2.06 us

profile of v2, /device:TPU:1, one launch (start us, length us, event | category | flops | bytes accessed | tf_op | source)
XLA Modules:
  0.0 56.8 jit_solution(773641555699360452)
XLA Ops:
  0.0 54.7 %span_attention_layer.1 = bf16[64,6144]{1,0:T(8,128)(2,1)} custom-call(bf16[64,3072]{1,0:T(8,128)(2,1)} %query.1, bf16[64,512]{1,0:T(8,128)(2,1)} %key.1, bf16[64,512]{1,0:T(8,128)(2,1)} %value.1, bf16[64,6144]{1,0:T(8,128)(2,1)} %residual.1, bf16[768,6144]{1,0:T(8,128)(2,1)} %weight.1, f32[4,6144]{1,0:T(4,128)} %gate_table.1, s32[32]{0:T(128)} %span_of_shard.1, ...), custom_call_target="tpu_custom_call" | custom-call | tf_op jit(solution)/shard_map/span_attention_layer/pallas_call | solution.py:568
  54.7 2.1 %copy.11 = bf16[64,6144]{1,0:T(8,128)(2,1)} copy(bf16[64,6144]{1,0:T(8,128)(2,1)} %span_attention_layer.1) | data formatting | bytes 1572864

commit v3 on v2

--- a/solution.py
+++ b/solution.py
@@ -41,8 +41,8 @@
 }
 COLUMNS = len(PLACE)
 STEPS = COLUMNS // 2
-FILL = {1: (0, 1)}
-AHEAD = 1
+FILL = {0: (0, 1), 1: (1, 2)}
+AHEAD = 2
 LEFT = STEPS - AHEAD
 LAG = 4
 FIRST = [(1, 0), (3, 0), (0, 1), (0, 3)]
@@ -197,7 +197,7 @@
     for step in (2, 1, 3, 0):
         for which in range(2):
             key_copy(step, which).start()
-    for step in (1, 3, 0):
+    for step in (1, 3, 2, 0):
         query_copy(step).start()
     for copy in local:
         copy.start()
@@ -268,9 +268,6 @@
     weight_b[...] = jnp.zeros(weight_b.shape, jnp.bfloat16)
     factor_a[...] = jnp.ones(factor_a.shape, jnp.float32)
     factor_b[...] = jnp.ones(factor_b.shape, jnp.float32)
-    for offset in FIRST:
-        arrive(*offset)
-
     scale = math.log2(math.e) / math.sqrt(HD)
 
     def take_queries(block):
@@ -435,11 +432,16 @@
             if n >= LAG:
                 use(n - LAG)
 
+    query_copy(0).wait()
+    take_queries(3)
     query_copy(1).wait_recv()
     query_copy(3).wait_recv()
-    query_copy(2).start()
     take_queries(0)
     take_queries(1)
+    query_copy(2).wait_recv()
+    take_queries(2)
+    for offset in FIRST:
+        arrive(*offset)
     side_wait(0)
     side_wait(1)
     score(0, 0, 0)
@@ -455,13 +457,6 @@
         return carry
 
     def early(i, carry):
-        @pl.when(i == 1)
-        def _():
-            query_copy(0).wait()
-            query_copy(2).wait_recv()
-            take_queries(2)
-            take_queries(3)
-
         for at, (low, high) in FILL.items():
 
             @pl.when(i == at)
@@ -560,12 +555,16 @@
         cross_copy(n).wait_send()
 
 
+def copy_kernel(src, dst):
+    dst[...] = src[...]
+
+
 def on_device(*arrays):
     anywhere = pl.BlockSpec(memory_space=pl.ANY)
     scalars = pl.BlockSpec(memory_space=pltpu.SMEM)
     bf16, f32 = jnp.bfloat16, jnp.float32
     dma = pltpu.SemaphoreType.DMA
-    return pl.pallas_call(
+    mixed = pl.pallas_call(
         layer_kernel,
         out_shape=jax.ShapeDtypeStruct((BLOCK, D), bf16),
         in_specs=[anywhere] * 6 + [scalars] * 3,
@@ -626,6 +625,14 @@
         ),
         name="span_attention_layer",
     )(*arrays)
+    return pl.pallas_call(
+        copy_kernel,
+        grid=(2,),
+        out_shape=jax.ShapeDtypeStruct((BLOCK, D), bf16),
+        in_specs=[pl.BlockSpec((BLOCK, D // 2), lambda i: (0, i))],
+        out_specs=pl.BlockSpec((BLOCK, D // 2), lambda i: (0, i)),
+        name="result",
+    )(mixed)
 
 
 def solution(mesh):

time: 57 us -> 56.7 us (level)
  local copies, waits for them, and re-layouts: 2.06 us -> 0 us
  Pallas kernels: 54.7 us -> 56.5 us
    unnamed x1 -> x0, local copies, waits for them, and re-layouts: 2.06 us -> none
    pallas_call x0 -> x1, Pallas kernels: none -> 1.91 us  [on_device(): pl.pallas_call(copy_kernel, grid=(2,), out_shape=jax.ShapeDtypeStruct((BL...]
where the time goes in v3:
time: 56.7 us; the launch traced here: 56.6 us
  Pallas kernels  56.5 us (100%)
    pallas_call x1, Pallas kernels, on_device(): pl.pallas_call(layer_kernel, out_shape=jax.ShapeDtypeStruct((BLOCK, D), b...  54.6 us
    pallas_call x1, Pallas kernels, on_device(): pl.pallas_call(copy_kernel, grid=(2,), out_shape=jax.ShapeDtypeStruct((BL...  1.91 us

profile of v3, /device:TPU:1, one launch (start us, length us, event | category | flops | bytes accessed | tf_op | source)
XLA Modules:
  0.0 56.6 jit_solution(9883389904992930368)
XLA Ops:
  0.0 54.6 %span_attention_layer.1.src = bf16[64,6144]{1,0:T(8,128)(2,1)} custom-call(bf16[64,3072]{1,0:T(8,128)(2,1)} %query.1, bf16[64,512]{1,0:T(8,128)(2,1)} %key.1, bf16[64,512]{1,0:T(8,128)(2,1)} %value.1, bf16[64,6144]{1,0:T(8,128)(2,1)} %residual.1, bf16[768,6144]{1,0:T(8,128)(2,1)} %weight.1, f32[4,6144]{1,0:T(4,128)} %gate_table.1, s32[32]{0:T(128)} %span_of_shard.1, ...), custom_call_target="tpu_custom_call" | custom-call | tf_op jit(solution)/shard_map/span_attention_layer/pallas_call | solution.py:567
  54.6 1.9 %result.1 = bf16[64,6144]{1,0:T(8,128)(2,1)} custom-call(bf16[64,6144]{1,0:T(8,128)(2,1)} %span_attention_layer.1.src), custom_call_target="tpu_custom_call" | custom-call | tf_op jit(solution)/shard_map/result/pallas_call | solution.py:628

commit v4 on v3

--- a/solution.py
+++ b/solution.py
@@ -45,16 +45,9 @@
 AHEAD = 2
 LEFT = STEPS - AHEAD
 LAG = 4
-FIRST = [(1, 0), (3, 0), (0, 1), (0, 3)]
-ARRIVE = {
-    1: [(1, 1), (3, 3), (3, 1), (1, 3), (0, 2)],
-    3: [(2, 1), (2, 3)],
-    5: [(2, 2)],
-}
-MIDDLE = {
-    0: [(2, 0)],
-    3: [(1, 2), (3, 2)],
-}
+FIRST = [(1, 0), (3, 0), (2, 0), (0, 1), (0, 3)]
+ARRIVE = {1: [(1, 1), (3, 3), (3, 1), (1, 3), (2, 1), (2, 3), (0, 2)], 4: [(1, 2), (3, 2), (2, 2)]}
+MIDDLE = {}
 
 
 def layer_kernel(
@@ -163,7 +156,7 @@
     barrier = pltpu.get_barrier_semaphore()
     peers = [in_column(1, core), in_column(2, core), in_column(3, core)]
     peers += [sibling, in_column(2, other)]
-    peers += [along(0, 1), along(0, -1), along(1, 1), along(1, -1)]
+    peers += [along(0, 1), along(0, -1), along(1, 1), along(1, -1), along(0, 2), along(1, 2)]
     for peer in peers:
         pl.semaphore_signal(barrier, inc=1, device_id=peer, device_id_type=MESH)
     top[...] = jnp.full(top.shape, NEG, jnp.float32)
@@ -229,11 +222,7 @@
         ways = []
         if second == 0:
             if first == 0:
-                ways += [(0, 1, None), (0, -1, None)]
-            if first == 1:
-                ways += [(0, 1, 0)]
-            if first == 3:
-                ways += [(0, -1, 1)]
+                ways += [(0, 1, None), (0, -1, None), (0, 2, None)]
             ways += [(1, 1, None), (1, -1, None)]
         elif second == 1:
             ways += [(1, 1, 0)]
@@ -243,7 +232,7 @@
 
     def arrive(first, second):
         at = place(first, second)
-        if (second if second else first) == 2:
+        if second == 2:
             for half in range(2):
                 spot = kv.at[at, core, half]
                 remote(spot, spot, g_send.at[at, half], g_recv.at[at, half], sibling).wait_recv()

time: 56.7 us -> 56.8 us (level)
  no operation moved by 1% of the time
where the time goes in v4:
time: 56.8 us; the launch traced here: 56.7 us
  Pallas kernels  56.7 us (100%)
    pallas_call x1, Pallas kernels, on_device(): pl.pallas_call(layer_kernel, out_shape=jax.ShapeDtypeStruct((BLOCK, D), b...  54.7 us
    pallas_call x1, Pallas kernels, on_device(): pl.pallas_call(copy_kernel, grid=(2,), out_shape=jax.ShapeDtypeStruct((BL...  1.91 us

profile of v4, /device:TPU:1, one launch (start us, length us, event | category | flops | bytes accessed | tf_op | source)
XLA Modules:
  0.0 56.7 jit_solution(13263716153827955213)
XLA Ops:
  0.0 54.7 %span_attention_layer.1.src = bf16[64,6144]{1,0:T(8,128)(2,1)} custom-call(bf16[64,3072]{1,0:T(8,128)(2,1)} %query.1, bf16[64,512]{1,0:T(8,128)(2,1)} %key.1, bf16[64,512]{1,0:T(8,128)(2,1)} %value.1, bf16[64,6144]{1,0:T(8,128)(2,1)} %residual.1, bf16[768,6144]{1,0:T(8,128)(2,1)} %weight.1, f32[4,6144]{1,0:T(4,128)} %gate_table.1, s32[32]{0:T(128)} %span_of_shard.1, ...), custom_call_target="tpu_custom_call" | custom-call | tf_op jit(solution)/shard_map/span_attention_layer/pallas_call | solution.py:556
  54.8 1.9 %result.1 = bf16[64,6144]{1,0:T(8,128)(2,1)} custom-call(bf16[64,6144]{1,0:T(8,128)(2,1)} %span_attention_layer.1.src), custom_call_target="tpu_custom_call" | custom-call | tf_op jit(solution)/shard_map/result/pallas_call | solution.py:617
